TPU v7x, 512 devices: a whole 4x8x8 slice. The times are simulated.
512 devices in a mesh: blk: 64 (over y_hi, z, core), acc: 4 (over x), tail: 2 (over y_lo).
Axes of the slice: x: 4, y: 8 (y_hi: 4, y_lo: 2; y = y_hi * 2 + y_lo), z: 8, core: 2. Of those that a mesh axis runs over, the one named last changes fastest.
Arguments:
- reciprocal_spectra: float32 [4, 2, 64, 4096], P(None, None, 'acc'), may hold values from -6 to 6
- divisor: float32 [128, 131072], P(('blk', 'tail'), 'acc'), may hold values from -1 to 1
Outputs:
- middle_product: float32 [128, 131072], P(('blk', 'tail'), 'acc')
All inputs are finite; a program needn't handle non-finite values.
Results may differ from a plain program's by a relative error of at most 0.0003.
Values sent between devices are 32-bit elements; how exact they have to be, the bound alone decides.
A program may use at most 64 MiB of HBM per device.

v0:
```python
import functools

import jax
import jax.numpy as jnp
import ml_dtypes
import numpy as np
from jax import lax
from jax.experimental import pallas as pl
from jax.experimental.pallas import tpu as pltpu
from jax.sharding import PartitionSpec as P

LENGTH = 262144
ACC = 4
ROWS = 16
OUTER = 64
MID = 32
LANES = 128
QUARTER = 256
HALF = QUARTER // 2
CHUNK = 4
CHUNKS = ROWS // CHUNK
ROUNDS = 4


def high_low(table):
    high = table.astype(ml_dtypes.bfloat16)
    low = (table - high.astype(np.float64)).astype(ml_dtypes.bfloat16)
    return high, low


def stacked_left(table):
    high, low = high_low(table)
    return np.concatenate(
        [
            np.concatenate([high, high], axis=-1),
            np.concatenate([low, np.zeros_like(low)], axis=-1),
        ],
        axis=-2,
    )


def root(product, modulus):
    angle = (product % modulus) * (-2.0 * np.pi / modulus)
    return np.cos(angle), np.sin(angle)


@functools.lru_cache(maxsize=None)
def tables():
    rows = np.arange(OUTER)
    limb = np.arange(OUTER)
    mid = np.arange(MID)
    lane = np.arange(LANES)
    kappa = np.concatenate([np.arange(0, MID, 2), np.arange(1, MID, 2)])
    bins = 2 * (lane % 64) + lane // 64
    first, first_back = [], []
    for place in range(ACC):
        own = rows[place * ROWS : (place + 1) * ROWS]
        real, imag = root(own[:, None] * limb[None, :], OUTER)
        first.append(stacked_left(np.concatenate([real, imag], axis=0)))
        order = [(place + 2) % ACC, (place + 1) % ACC, (place + 3) % ACC, place]
        kept = np.concatenate([np.arange(8 * q, 8 * q + 8) for q in order])
        real, imag = root(kept[:, None] * own[None, :], OUTER)
        first_back.append(stacked_left(np.concatenate([real, imag], axis=1) / LENGTH))
    freq = rows[:, None] + OUTER * kappa[None, :]
    real, imag = root(freq[:, :, None] * mid[None, None, :], 2048)
    second = stacked_left(
        np.concatenate(
            [np.concatenate([real, -imag], axis=2), np.concatenate([imag, real], axis=2)], axis=1
        )
    )
    real, imag = real.transpose(0, 2, 1), -imag.transpose(0, 2, 1)
    second_back = stacked_left(
        np.concatenate(
            [np.concatenate([real, -imag], axis=2), np.concatenate([imag, real], axis=2)], axis=1
        )
    )
    real, imag = root(freq[:, :, None] * lane[None, None, :], LENGTH)
    twiddle = np.stack([real, imag], axis=1).astype(np.float32)
    real, imag = root(lane[:, None] * bins[None, :], LANES)
    third = np.stack(
        high_low(
            np.concatenate(
                [np.concatenate([real, imag], axis=1), np.concatenate([-imag, real], axis=1)], axis=0
            )
        )
    )
    real, imag = real.T, -imag.T
    third_back = np.stack(
        high_low(
            np.concatenate(
                [np.concatenate([real, imag], axis=1), np.concatenate([-imag, real], axis=1)], axis=0
            )
        )
    )
    return (
        np.stack(first),
        second,
        twiddle,
        third,
        third_back,
        second_back,
        np.stack(first_back),
    )


def split(value):
    high = value.astype(jnp.bfloat16)
    low = (value - high.astype(jnp.float32)).astype(jnp.bfloat16)
    return high, low


def dot(first, second):
    return jnp.dot(first, second, preferred_element_type=jnp.float32)


def left_product(stacked, value):
    high, low = split(value)
    both = dot(stacked, jnp.concatenate([high, low], axis=0))
    rows = both.shape[0] // 2
    return both[:rows] + both[rows:]


def right_product(value, table):
    high, low = split(value)
    rows = value.shape[0]
    both = dot(jnp.concatenate([high, low], axis=0), table[0])
    return both[:rows] + both[rows:] + dot(high, table[1])


def exchanged(value, lower):
    top, bottom = value[: MID // 2], value[MID // 2 :]
    return jnp.concatenate(
        [
            jnp.where(lower, top, pltpu.roll(bottom, 64, 1)),
            jnp.where(lower, pltpu.roll(top, 64, 1), bottom),
        ],
        axis=0,
    )


def kernel(
    blocks,
    recip_hbm,
    limbs_hbm,
    first_hbm,
    second_hbm,
    twiddle_hbm,
    third_ref,
    third_back_ref,
    second_back_hbm,
    first_back_hbm,
    out_ref,
    recip,
    limbs,
    first,
    second,
    twiddle,
    second_back,
    first_back,
    mixed,
    spectra,
    total,
    back,
    result,
    transit,
    arrived,
    local_sem,
    over_send,
    over_recv,
    gather_send,
    gather_recv,
    ring_send,
    ring_recv,
    sum_send,
    sum_recv,
):
    blk = lax.axis_index("blk")
    acc = lax.axis_index("acc")
    tail = lax.axis_index("tail")
    right = {"blk": blk, "acc": lax.rem(acc + 1, ACC), "tail": tail}
    left = {"blk": blk, "acc": lax.rem(acc + ACC - 1, ACC), "tail": tail}
    later = {"blk": lax.rem(blk + tail, blocks), "acc": acc, "tail": 1 - tail}
    earlier = {"blk": lax.rem(blk + blocks - 1 + tail, blocks), "acc": acc, "tail": 1 - tail}
    onward = {"blk": lax.rem(blk + 1, blocks), "acc": acc, "tail": tail}
    backward = {"blk": lax.rem(blk + blocks - 1, blocks), "acc": acc, "tail": tail}

    def remote(src, dst, send_sem, recv_sem, device):
        return pltpu.make_async_remote_copy(
            src_ref=src,
            dst_ref=dst,
            send_sem=send_sem,
            recv_sem=recv_sem,
            device_id=device,
            device_id_type=pl.DeviceIdType.MESH,
        )

    def quarter(part, owner, start, size):
        first_row = pl.multiple_of((part * ACC + owner) * QUARTER + start, HALF)
        return limbs.at[pl.ds(first_row, size)]

    barrier = pltpu.get_barrier_semaphore()
    for device in (right, left, later, earlier, onward, backward):
        pl.semaphore_signal(barrier, inc=1, device_id=device, device_id_type=pl.DeviceIdType.MESH)
    own_rows = pl.ds(acc * ROWS, ROWS)
    own_limbs = pltpu.make_async_copy(limbs_hbm, quarter(0, acc, 0, QUARTER), local_sem.at[0])
    local = [
        pltpu.make_async_copy(first_hbm.at[acc], first, local_sem.at[1]),
        pltpu.make_async_copy(second_hbm.at[own_rows], second, local_sem.at[2]),
        pltpu.make_async_copy(twiddle_hbm.at[own_rows], twiddle, local_sem.at[3]),
        pltpu.make_async_copy(second_back_hbm.at[own_rows], second_back, local_sem.at[4]),
        pltpu.make_async_copy(first_back_hbm.at[acc], first_back, local_sem.at[5]),
        pltpu.make_async_copy(recip_hbm, recip, local_sem.at[6]),
    ]
    own_limbs.start()
    for copy in local:
        copy.start()
    own_limbs.wait()
    pl.semaphore_wait(barrier, 6)

    over = remote(
        quarter(0, acc, 0, QUARTER),
        quarter(1, acc, 0, QUARTER),
        over_send.at[0],
        over_recv.at[0],
        later,
    )
    over.start()

    def gather(part, step, owner, start, device):
        ref = quarter(part, owner, start, HALF)
        return remote(ref, ref, gather_send.at[part, step], gather_recv.at[part, step], device)

    from_left = lax.rem(acc + ACC - 1, ACC)
    from_right = lax.rem(acc + 1, ACC)
    copies = []

    def spread(part):
        steps = [
            gather(part, 0, acc, 0, right),
            gather(part, 1, acc, HALF, left),
            gather(part, 2, acc, HALF, right),
            gather(part, 3, acc, 0, left),
        ]
        for copy in steps:
            copy.start()
        return steps

    def pass_on(part, steps):
        steps[0].wait_recv()
        to_right = gather(part, 4, from_left, 0, right)
        to_right.start()
        steps[1].wait_recv()
        to_left = gather(part, 5, from_right, HALF, left)
        to_left.start()
        return [to_right, to_left]

    own_steps = spread(0)
    over.wait_recv()
    earlier_steps = spread(1)
    own_steps += pass_on(0, own_steps)
    earlier_steps += pass_on(1, earlier_steps)
    for copy in own_steps[2:] + earlier_steps[2:]:
        copy.wait_recv()
    for copy in local:
        copy.wait()

    lower = lax.broadcasted_iota(jnp.int32, (MID // 2, LANES), 1) < 64

    def first_step(pair, carry):
        values = [limbs[pl.ds(2 * pair + side, OUTER, stride=MID)] for side in range(2)]
        product = left_product(first[...], jnp.concatenate(values, axis=1))
        for side in range(2):
            start = pl.multiple_of((2 * pair + side) * 2 * ROWS, 2 * ROWS)
            mixed[pl.ds(start, 2 * ROWS)] = product[:, side * LANES : (side + 1) * LANES]
        return carry

    lax.fori_loop(0, MID // 2, first_step, 0)

    def ring(step, chunk):
        rows = pl.ds(chunk * CHUNK, CHUNK)
        return remote(
            spectra.at[step, rows],
            spectra.at[step + 1, rows],
            ring_send.at[step, chunk],
            ring_recv.at[step, chunk],
            onward,
        )

    def forward(chunk, carry):
        reals, imags = [], []
        for place in range(CHUNK):
            row = chunk * CHUNK + place
            value = jnp.concatenate(
                [
                    mixed[pl.ds(row, MID, stride=2 * ROWS)],
                    mixed[pl.ds(ROWS + row, MID, stride=2 * ROWS)],
                ],
                axis=0,
            )
            product = left_product(second[row], value)
            real, imag = product[:MID], product[MID:]
            turn_real, turn_imag = twiddle[row, 0], twiddle[row, 1]
            reals.append(real * turn_real - imag * turn_imag)
            imags.append(real * turn_imag + imag * turn_real)
        value = jnp.concatenate(
            [jnp.concatenate(reals, axis=0), jnp.concatenate(imags, axis=0)], axis=1
        )
        product = right_product(value, third_ref)
        for place in range(CHUNK):
            rows = product[place * MID : (place + 1) * MID]
            spectra[0, chunk * CHUNK + place, 0] = exchanged(rows[:, :LANES], lower)
            spectra[0, chunk * CHUNK + place, 1] = exchanged(rows[:, LANES:], lower)
        ring(0, chunk).start()
        return carry

    lax.fori_loop(0, CHUNKS, forward, 0)

    def term(step, row, chunk, place):
        start = step * 1024 + (chunk // 2) * 256 + lax.rem(chunk, 2) * CHUNK + place
        recip_real = recip[pl.ds(start, MID, stride=8)]
        recip_imag = recip[pl.ds(start + 512, MID, stride=8)]
        real, imag = spectra[step, row, 0], spectra[step, row, 1]
        return recip_real * real - recip_imag * imag, recip_real * imag + recip_imag * real

    def arrive_first(chunk, carry):
        ring(0, chunk).wait_recv()
        ring(1, chunk).start()
        for place in range(CHUNK):
            row = chunk * CHUNK + place
            real, imag = term(0, row, chunk, place)
            more_real, more_imag = term(1, row, chunk, place)
            total[row, 0] = real + more_real
            total[row, 1] = imag + more_imag
        return carry

    lax.fori_loop(0, CHUNKS, arrive_first, 0)

    def arrive_second(chunk, carry):
        ring(1, chunk).wait_recv()
        ring(2, chunk).start()
        for place in range(CHUNK):
            row = chunk * CHUNK + place
            real, imag = term(2, row, chunk, place)
            total[row, 0] += real
            total[row, 1] += imag
        return carry

    lax.fori_loop(0, CHUNKS, arrive_second, 0)

    def arrive_third(chunk, carry):
        ring(2, chunk).wait_recv()
        reals, imags = [], []
        for place in range(CHUNK):
            row = chunk * CHUNK + place
            real, imag = term(3, row, chunk, place)
            reals.append(exchanged(total[row, 0] + real, lower))
            imags.append(exchanged(total[row, 1] + imag, lower))
        value = jnp.concatenate(
            [jnp.concatenate(reals, axis=0), jnp.concatenate(imags, axis=0)], axis=1
        )
        product = right_product(value, third_back_ref)
        for place in range(CHUNK):
            row = chunk * CHUNK + place
            real = product[place * MID : (place + 1) * MID, :LANES]
            imag = product[place * MID : (place + 1) * MID, LANES:]
            turn_real, turn_imag = twiddle[row, 0], twiddle[row, 1]
            turned = jnp.concatenate(
                [real * turn_real + imag * turn_imag, imag * turn_real - real * turn_imag], axis=0
            )
            unmixed = left_product(second_back[row], turned)
            back[pl.ds(row, MID, stride=2 * ROWS)] = unmixed[:MID]
            back[pl.ds(ROWS + row, MID, stride=2 * ROWS)] = unmixed[MID:]
        return carry

    lax.fori_loop(0, CHUNKS, arrive_third, 0)

    def last_step(pair, carry):
        values = []
        for side in range(2):
            start = pl.multiple_of((2 * pair + side) * 2 * ROWS, 2 * ROWS)
            values.append(back[pl.ds(start, 2 * ROWS)])
        product = left_product(first_back[...], jnp.concatenate(values, axis=1))
        for side in range(2):
            result[pl.ds(2 * pair + side, MID, stride=MID)] = product[
                :, side * LANES : (side + 1) * LANES
            ]
        return carry

    lax.fori_loop(0, MID // 2, last_step, 0)

    def part(place, start):
        return result.at[pl.ds(place * QUARTER + start, HALF)]

    to_right = remote(part(0, 0), transit.at[0], sum_send.at[0], sum_recv.at[0], right)
    to_left = remote(part(0, HALF), transit.at[1], sum_send.at[1], sum_recv.at[1], left)
    plain_right = remote(part(1, HALF), arrived.at[0], sum_send.at[2], sum_recv.at[2], right)
    plain_left = remote(part(2, 0), arrived.at[1], sum_send.at[3], sum_recv.at[3], left)
    summed_right = remote(part(1, 0), arrived.at[2], sum_send.at[4], sum_recv.at[4], right)
    summed_left = remote(part(2, HALF), arrived.at[3], sum_send.at[5], sum_recv.at[5], left)
    to_right.start()
    to_left.start()
    plain_right.start()
    plain_left.start()
    to_right.wait_recv()
    result[QUARTER : QUARTER + HALF] += transit[0]
    summed_right.start()
    to_left.wait_recv()
    result[2 * QUARTER + HALF : 3 * QUARTER] += transit[1]
    summed_left.start()
    plain_right.wait_recv()
    plain_left.wait_recv()
    summed_right.wait_recv()
    out_ref[:HALF] = result[3 * QUARTER : 3 * QUARTER + HALF] + arrived[1] + arrived[2]
    summed_left.wait_recv()
    out_ref[HALF:] = result[3 * QUARTER + HALF :] + arrived[0] + arrived[3]

    sent = [over, *own_steps, *earlier_steps]
    sent += [to_right, to_left, plain_right, plain_left, summed_right, summed_left]
    for copy in sent:
        copy.wait_send()

    def drain(chunk, carry):
        for step in range(ROUNDS - 1):
            ring(step, chunk).wait_send()
        return carry

    lax.fori_loop(0, CHUNKS, drain, 0)


def per_device(blocks, reciprocal_spectra, divisor):
    recip = reciprocal_spectra.reshape(ROUNDS, 2, 2, 8, MID, LANES)
    recip = recip.transpose(0, 1, 2, 4, 3, 5).reshape(ROUNDS * 1024, LANES)
    limbs = divisor.reshape(QUARTER, LANES)
    constants = [jnp.asarray(table) for table in tables()]
    first, second, twiddle, third, third_back, second_back, first_back = constants
    anywhere = pl.BlockSpec(memory_space=pl.ANY)
    vmem = pl.BlockSpec(memory_space=pltpu.VMEM)
    out = pl.pallas_call(
        functools.partial(kernel, blocks),
        out_shape=jax.ShapeDtypeStruct((QUARTER, LANES), jnp.float32),
        in_specs=[anywhere] * 5 + [vmem] * 2 + [anywhere] * 2,
        out_specs=vmem,
        scratch_shapes=[
            pltpu.VMEM((ROUNDS * 1024, LANES), jnp.float32),
            pltpu.VMEM((2 * ACC * QUARTER, LANES), jnp.float32),
            pltpu.VMEM(first.shape[1:], jnp.bfloat16),
            pltpu.VMEM((ROWS, *second.shape[1:]), jnp.bfloat16),
            pltpu.VMEM((ROWS, *twiddle.shape[1:]), jnp.float32),
            pltpu.VMEM((ROWS, *second_back.shape[1:]), jnp.bfloat16),
            pltpu.VMEM(first_back.shape[1:], jnp.bfloat16),
            pltpu.VMEM((MID * 2 * ROWS, LANES), jnp.float32),
            pltpu.VMEM((ROUNDS, ROWS, 2, MID, LANES), jnp.float32),
            pltpu.VMEM((ROWS, 2, MID, LANES), jnp.float32),
            pltpu.VMEM((MID * 2 * ROWS, LANES), jnp.float32),
            pltpu.VMEM((ACC * QUARTER, LANES), jnp.float32),
            pltpu.VMEM((2, HALF, LANES), jnp.float32),
            pltpu.VMEM((4, HALF, LANES), jnp.float32),
            pltpu.SemaphoreType.DMA((7,)),
            pltpu.SemaphoreType.DMA((1,)),
            pltpu.SemaphoreType.DMA((1,)),
            pltpu.SemaphoreType.DMA((2, 6)),
            pltpu.SemaphoreType.DMA((2, 6)),
            pltpu.SemaphoreType.DMA((ROUNDS - 1, CHUNKS)),
            pltpu.SemaphoreType.DMA((ROUNDS - 1, CHUNKS)),
            pltpu.SemaphoreType.DMA((6,)),
            pltpu.SemaphoreType.DMA((6,)),
        ],
        compiler_params=pltpu.CompilerParams(
            collective_id=0, has_side_effects=True, vmem_limit_bytes=60 * 1024 * 1024
        ),
    )(recip, limbs, first, second, twiddle, third, third_back, second_back, first_back)
    return out.reshape(1, QUARTER * LANES)


def solution(mesh):
    in_specs = (P(None, None, "acc", None), P(("blk", "tail"), "acc"))
    out_specs = P(("blk", "tail"), "acc")
    return jax.shard_map(
        functools.partial(per_device, mesh.shape["blk"]),
        mesh=mesh,
        in_specs=in_specs,
        out_specs=out_specs,
        check_vma=False,
    )
```

profile of v0, /device:TPU:2, one launch (start us, length us, event | category | flops | bytes accessed | tf_op | source)
XLA Modules:
  0.0 78.3 jit_solution(1817350098274577931)
XLA Ops:
  0.0 76.8 %shard_map.91 = f32[256,128]{1,0:T(8,128)} custom-call(f32[4096,128]{1,0:T(8,128)} %bitcast.7, f32[256,128]{1,0:T(8,128)} %bitcast.9, bf16[4,64,128]{2,1,0:T(8,128)(2,1)} %constant.14.clone.first_hbm, bf16[64,128,128]{2,1,0:T(8,128)(2,1)} %constant.15.clone.second_hbm, f32[64,2,32,128]{3,2,1,0:T(8,128)} %constant.16.clone.twiddle_hbm, ...), custom_call_target="tpu_custom_call" | custom-call | tf_op jit(solution)/shard_map/pallas_call | solution.py:438
  76.8 1.6 %copy.11 = f32[1,32768]{1,0:T(1,128)} copy(f32[1,32768]{1,0:T(1,128)} %bitcast.8) | data formatting | bytes 262144
where the time goes:
time: 78.5 us; the launch traced here: 78.3 us
  Pallas kernels  76.8 us (98%)
  local copies, waits for them, and re-layouts  1.57 us (2%)
    pallas_call x1, Pallas kernels, per_device(): pl.pallas_call(functools.partial(kernel, blocks), out_shape=jax.ShapeDtyp...  76.8 us

commit v1 on v0

--- a/solution.py
+++ b/solution.py
@@ -11,15 +11,19 @@
 
 LENGTH = 262144
 ACC = 4
-ROWS = 16
+OWNED = 16
+ROWS = 9
+PADDED = 32
 OUTER = 64
 MID = 32
 LANES = 128
 QUARTER = 256
 HALF = QUARTER // 2
-CHUNK = 4
+CHUNK = 3
 CHUNKS = ROWS // CHUNK
 ROUNDS = 4
+CORES = 2
+CYCLE = 16
 
 
 def high_low(table):
@@ -54,13 +58,15 @@
     bins = 2 * (lane % 64) + lane // 64
     first, first_back = [], []
     for place in range(ACC):
-        own = rows[place * ROWS : (place + 1) * ROWS]
+        own = rows[place * OWNED : place * OWNED + ROWS]
         real, imag = root(own[:, None] * limb[None, :], OUTER)
-        first.append(stacked_left(np.concatenate([real, imag], axis=0)))
+        empty = np.zeros((PADDED - 2 * ROWS, OUTER))
+        first.append(stacked_left(np.concatenate([real, imag, empty], axis=0)))
         order = [(place + 2) % ACC, (place + 1) % ACC, (place + 3) % ACC, place]
         kept = np.concatenate([np.arange(8 * q, 8 * q + 8) for q in order])
         real, imag = root(kept[:, None] * own[None, :], OUTER)
-        first_back.append(stacked_left(np.concatenate([real, imag], axis=1) / LENGTH))
+        empty = np.zeros((len(kept), PADDED - 2 * ROWS))
+        first_back.append(stacked_left(np.concatenate([real, imag, empty], axis=1) / LENGTH))
     freq = rows[:, None] + OUTER * kappa[None, :]
     real, imag = root(freq[:, :, None] * mid[None, None, :], 2048)
     second = stacked_left(
@@ -100,6 +106,7 @@
         third_back,
         second_back,
         np.stack(first_back),
+        np.concatenate([np.eye(LANES)[::-1]] * 2, axis=0).astype(ml_dtypes.bfloat16),
     )
 
 
@@ -147,10 +154,14 @@
     twiddle_hbm,
     third_ref,
     third_back_ref,
+    flip_ref,
     second_back_hbm,
     first_back_hbm,
     out_ref,
     recip,
+    paired,
+    flipped,
+    weights,
     limbs,
     first,
     second,
@@ -159,7 +170,6 @@
     first_back,
     mixed,
     spectra,
-    total,
     back,
     result,
     transit,
@@ -169,6 +179,8 @@
     over_recv,
     gather_send,
     gather_recv,
+    share_send,
+    share_recv,
     ring_send,
     ring_recv,
     sum_send,
@@ -183,6 +195,14 @@
     earlier = {"blk": lax.rem(blk + blocks - 1 + tail, blocks), "acc": acc, "tail": 1 - tail}
     onward = {"blk": lax.rem(blk + 1, blocks), "acc": acc, "tail": tail}
     backward = {"blk": lax.rem(blk + blocks - 1, blocks), "acc": acc, "tail": tail}
+    partner = {"blk": blk, "acc": ACC - 1 - acc, "tail": tail}
+    cycle = min(CYCLE, blocks)
+    spot = lax.rem(blk, cycle)
+    core = lax.rem(blk, CORES)
+    parity = lax.rem(spot // CORES, 2)
+    mate = {"blk": blk + 1 - 2 * core, "acc": acc, "tail": tail}
+    below = {"blk": blk - spot + lax.rem(spot + cycle - CORES, cycle), "acc": acc, "tail": tail}
+    above = {"blk": blk - spot + lax.rem(spot + CORES, cycle), "acc": acc, "tail": tail}
 
     def remote(src, dst, send_sem, recv_sem, device):
         return pltpu.make_async_remote_copy(
@@ -199,9 +219,9 @@
         return limbs.at[pl.ds(first_row, size)]
 
     barrier = pltpu.get_barrier_semaphore()
-    for device in (right, left, later, earlier, onward, backward):
+    for device in (right, left, later, earlier, onward, backward, below, above):
         pl.semaphore_signal(barrier, inc=1, device_id=device, device_id_type=pl.DeviceIdType.MESH)
-    own_rows = pl.ds(acc * ROWS, ROWS)
+    own_rows = pl.ds(acc * OWNED, ROWS)
     own_limbs = pltpu.make_async_copy(limbs_hbm, quarter(0, acc, 0, QUARTER), local_sem.at[0])
     local = [
         pltpu.make_async_copy(first_hbm.at[acc], first, local_sem.at[1]),
@@ -215,7 +235,14 @@
     for copy in local:
         copy.start()
     own_limbs.wait()
-    pl.semaphore_wait(barrier, 6)
+
+    def clear(mid, carry):
+        start = pl.multiple_of(mid * PADDED, PADDED)
+        back[pl.ds(start + 16, PADDED - 16)] = jnp.zeros((PADDED - 16, LANES), jnp.float32)
+        return carry
+
+    lax.fori_loop(0, MID, clear, 0)
+    pl.semaphore_wait(barrier, 8)
 
     over = remote(
         quarter(0, acc, 0, QUARTER),
@@ -232,7 +259,6 @@
 
     from_left = lax.rem(acc + ACC - 1, ACC)
     from_right = lax.rem(acc + 1, ACC)
-    copies = []
 
     def spread(part):
         steps = [
@@ -259,6 +285,30 @@
     earlier_steps = spread(1)
     own_steps += pass_on(0, own_steps)
     earlier_steps += pass_on(1, earlier_steps)
+
+    def share(step, source, round_index, device):
+        found = []
+        for side in range(2):
+            start = pl.multiple_of(round_index * 1024 + side * 512 + 256, 256)
+            slot = paired.at[round_index, side]
+            found.append(
+                remote(
+                    recip_hbm.at[pl.ds(start, 256)] if source is None else slot,
+                    slot,
+                    share_send.at[step, side],
+                    share_recv.at[step, side],
+                    device,
+                )
+            )
+        return found
+
+    own_round = parity * 2 + core
+    fetched = share(0, None, own_round, partner)
+    to_mate = share(1, paired, own_round, mate)
+    to_below = share(2, paired, own_round, below)
+    relayed = share(3, paired, (1 - parity) * 2 + core, mate)
+    for copy in fetched:
+        copy.start()
     for copy in own_steps[2:] + earlier_steps[2:]:
         copy.wait_recv()
     for copy in local:
@@ -270,21 +320,24 @@
         values = [limbs[pl.ds(2 * pair + side, OUTER, stride=MID)] for side in range(2)]
         product = left_product(first[...], jnp.concatenate(values, axis=1))
         for side in range(2):
-            start = pl.multiple_of((2 * pair + side) * 2 * ROWS, 2 * ROWS)
-            mixed[pl.ds(start, 2 * ROWS)] = product[:, side * LANES : (side + 1) * LANES]
+            start = pl.multiple_of((2 * pair + side) * PADDED, PADDED)
+            mixed[pl.ds(start, PADDED)] = product[:, side * LANES : (side + 1) * LANES]
         return carry
 
     lax.fori_loop(0, MID // 2, first_step, 0)
 
     def ring(step, chunk):
         rows = pl.ds(chunk * CHUNK, CHUNK)
-        return remote(
-            spectra.at[step, rows],
-            spectra.at[step + 1, rows],
-            ring_send.at[step, chunk],
-            ring_recv.at[step, chunk],
-            onward,
-        )
+        return [
+            remote(
+                spectra.at[step, side, rows],
+                spectra.at[step + 1, side, rows],
+                ring_send.at[step, chunk, side],
+                ring_recv.at[step, chunk, side],
+                onward,
+            )
+            for side in range(2)
+        ]
 
     def forward(chunk, carry):
         reals, imags = [], []
@@ -292,8 +345,8 @@
             row = chunk * CHUNK + place
             value = jnp.concatenate(
                 [
-                    mixed[pl.ds(row, MID, stride=2 * ROWS)],
-                    mixed[pl.ds(ROWS + row, MID, stride=2 * ROWS)],
+                    mixed[pl.ds(row, MID, stride=PADDED)],
+                    mixed[pl.ds(ROWS + row, MID, stride=PADDED)],
                 ],
                 axis=0,
             )
@@ -308,53 +361,70 @@
         product = right_product(value, third_ref)
         for place in range(CHUNK):
             rows = product[place * MID : (place + 1) * MID]
-            spectra[0, chunk * CHUNK + place, 0] = exchanged(rows[:, :LANES], lower)
-            spectra[0, chunk * CHUNK + place, 1] = exchanged(rows[:, LANES:], lower)
-        ring(0, chunk).start()
+            spectra[0, 0, chunk * CHUNK + place] = exchanged(rows[:, :LANES], lower)
+            spectra[0, 1, chunk * CHUNK + place] = exchanged(rows[:, LANES:], lower)
+        for copy in ring(0, chunk):
+            copy.start()
         return carry
 
     lax.fori_loop(0, CHUNKS, forward, 0)
 
-    def term(step, row, chunk, place):
-        start = step * 1024 + (chunk // 2) * 256 + lax.rem(chunk, 2) * CHUNK + place
-        recip_real = recip[pl.ds(start, MID, stride=8)]
-        recip_imag = recip[pl.ds(start + 512, MID, stride=8)]
-        real, imag = spectra[step, row, 0], spectra[step, row, 1]
-        return recip_real * real - recip_imag * imag, recip_real * imag + recip_imag * real
-
-    def arrive_first(chunk, carry):
-        ring(0, chunk).wait_recv()
-        ring(1, chunk).start()
-        for place in range(CHUNK):
-            row = chunk * CHUNK + place
-            real, imag = term(0, row, chunk, place)
-            more_real, more_imag = term(1, row, chunk, place)
-            total[row, 0] = real + more_real
-            total[row, 1] = imag + more_imag
-        return carry
-
-    lax.fori_loop(0, CHUNKS, arrive_first, 0)
-
-    def arrive_second(chunk, carry):
-        ring(1, chunk).wait_recv()
-        ring(2, chunk).start()
-        for place in range(CHUNK):
-            row = chunk * CHUNK + place
-            real, imag = term(2, row, chunk, place)
-            total[row, 0] += real
-            total[row, 1] += imag
-        return carry
-
-    lax.fori_loop(0, CHUNKS, arrive_second, 0)
-
-    def arrive_third(chunk, carry):
-        ring(2, chunk).wait_recv()
+    for side in range(2):
+        fetched[side].wait_recv()
+        to_mate[side].start()
+        to_below[side].start()
+
+    def pass_ring(step):
+        def body(chunk, carry):
+            for come, go in zip(ring(step, chunk), ring(step + 1, chunk)):
+                come.wait_recv()
+                go.start()
+            return carry
+
+        lax.fori_loop(0, CHUNKS, body, 0)
+
+    pass_ring(0)
+    for side in range(2):
+        to_below[side].wait_recv()
+        relayed[side].start()
+    pass_ring(1)
+    for side in range(2):
+        to_mate[side].wait_recv()
+        relayed[side].wait_recv()
+
+    def weigh(step, carry):
+        for side in range(2):
+            high, low = split(paired[step, side])
+            turned = dot(jnp.concatenate([high, low], axis=1), flip_ref[...])
+            for group in range(MID):
+                flipped[side, pl.ds((MID - 1 - group) * 8, 8)] = turned[group * 8 : group * 8 + 8]
+            start = step * 1024 + side * 512
+            weights[step, side, 0] = recip[pl.ds(start, MID, stride=8)]
+            weights[step, side, ROWS - 1] = recip[pl.ds(start + 256, MID, stride=8)]
+            for row in range(1, ROWS - 1):
+                own = recip[pl.ds(start + row, MID, stride=8)]
+                other = flipped[side, pl.ds(8 - row, MID, stride=8)]
+                weights[step, side, row] = own + other if side == 0 else own - other
+        return carry
+
+    lax.fori_loop(0, ROUNDS, weigh, 0)
+
+    def arrive(chunk, carry):
+        for copy in ring(2, chunk):
+            copy.wait_recv()
         reals, imags = [], []
         for place in range(CHUNK):
             row = chunk * CHUNK + place
-            real, imag = term(3, row, chunk, place)
-            reals.append(exchanged(total[row, 0] + real, lower))
-            imags.append(exchanged(total[row, 1] + imag, lower))
+            total_real = total_imag = None
+            for step in range(ROUNDS):
+                weight_real, weight_imag = weights[step, 0, row], weights[step, 1, row]
+                real, imag = spectra[step, 0, row], spectra[step, 1, row]
+                term_real = weight_real * real - weight_imag * imag
+                term_imag = weight_real * imag + weight_imag * real
+                total_real = term_real if step == 0 else total_real + term_real
+                total_imag = term_imag if step == 0 else total_imag + term_imag
+            reals.append(exchanged(total_real, lower))
+            imags.append(exchanged(total_imag, lower))
         value = jnp.concatenate(
             [jnp.concatenate(reals, axis=0), jnp.concatenate(imags, axis=0)], axis=1
         )
@@ -368,17 +438,17 @@
                 [real * turn_real + imag * turn_imag, imag * turn_real - real * turn_imag], axis=0
             )
             unmixed = left_product(second_back[row], turned)
-            back[pl.ds(row, MID, stride=2 * ROWS)] = unmixed[:MID]
-            back[pl.ds(ROWS + row, MID, stride=2 * ROWS)] = unmixed[MID:]
-        return carry
-
-    lax.fori_loop(0, CHUNKS, arrive_third, 0)
+            back[pl.ds(row, MID, stride=PADDED)] = unmixed[:MID]
+            back[pl.ds(ROWS + row, MID, stride=PADDED)] = unmixed[MID:]
+        return carry
+
+    lax.fori_loop(0, CHUNKS, arrive, 0)
 
     def last_step(pair, carry):
         values = []
         for side in range(2):
-            start = pl.multiple_of((2 * pair + side) * 2 * ROWS, 2 * ROWS)
-            values.append(back[pl.ds(start, 2 * ROWS)])
+            start = pl.multiple_of((2 * pair + side) * PADDED, PADDED)
+            values.append(back[pl.ds(start, PADDED)])
         product = left_product(first_back[...], jnp.concatenate(values, axis=1))
         for side in range(2):
             result[pl.ds(2 * pair + side, MID, stride=MID)] = product[
@@ -415,13 +485,15 @@
     out_ref[HALF:] = result[3 * QUARTER + HALF :] + arrived[0] + arrived[3]
 
     sent = [over, *own_steps, *earlier_steps]
+    sent += [*fetched, *to_mate, *to_below, *relayed]
     sent += [to_right, to_left, plain_right, plain_left, summed_right, summed_left]
     for copy in sent:
         copy.wait_send()
 
     def drain(chunk, carry):
         for step in range(ROUNDS - 1):
-            ring(step, chunk).wait_send()
+            for copy in ring(step, chunk):
+                copy.wait_send()
         return carry
 
     lax.fori_loop(0, CHUNKS, drain, 0)
@@ -432,26 +504,28 @@
     recip = recip.transpose(0, 1, 2, 4, 3, 5).reshape(ROUNDS * 1024, LANES)
     limbs = divisor.reshape(QUARTER, LANES)
     constants = [jnp.asarray(table) for table in tables()]
-    first, second, twiddle, third, third_back, second_back, first_back = constants
+    first, second, twiddle, third, third_back, second_back, first_back, flip = constants
     anywhere = pl.BlockSpec(memory_space=pl.ANY)
     vmem = pl.BlockSpec(memory_space=pltpu.VMEM)
     out = pl.pallas_call(
         functools.partial(kernel, blocks),
         out_shape=jax.ShapeDtypeStruct((QUARTER, LANES), jnp.float32),
-        in_specs=[anywhere] * 5 + [vmem] * 2 + [anywhere] * 2,
+        in_specs=[anywhere] * 5 + [vmem] * 3 + [anywhere] * 2,
         out_specs=vmem,
         scratch_shapes=[
             pltpu.VMEM((ROUNDS * 1024, LANES), jnp.float32),
+            pltpu.VMEM((ROUNDS, 2, QUARTER, LANES), jnp.float32),
+            pltpu.VMEM((2, QUARTER, LANES), jnp.float32),
+            pltpu.VMEM((ROUNDS, 2, ROWS, MID, LANES), jnp.float32),
             pltpu.VMEM((2 * ACC * QUARTER, LANES), jnp.float32),
             pltpu.VMEM(first.shape[1:], jnp.bfloat16),
             pltpu.VMEM((ROWS, *second.shape[1:]), jnp.bfloat16),
             pltpu.VMEM((ROWS, *twiddle.shape[1:]), jnp.float32),
             pltpu.VMEM((ROWS, *second_back.shape[1:]), jnp.bfloat16),
             pltpu.VMEM(first_back.shape[1:], jnp.bfloat16),
-            pltpu.VMEM((MID * 2 * ROWS, LANES), jnp.float32),
-            pltpu.VMEM((ROUNDS, ROWS, 2, MID, LANES), jnp.float32),
-            pltpu.VMEM((ROWS, 2, MID, LANES), jnp.float32),
-            pltpu.VMEM((MID * 2 * ROWS, LANES), jnp.float32),
+            pltpu.VMEM((MID * PADDED, LANES), jnp.float32),
+            pltpu.VMEM((ROUNDS, 2, ROWS, MID, LANES), jnp.float32),
+            pltpu.VMEM((MID * PADDED, LANES), jnp.float32),
             pltpu.VMEM((ACC * QUARTER, LANES), jnp.float32),
             pltpu.VMEM((2, HALF, LANES), jnp.float32),
             pltpu.VMEM((4, HALF, LANES), jnp.float32),
@@ -460,15 +534,17 @@
             pltpu.SemaphoreType.DMA((1,)),
             pltpu.SemaphoreType.DMA((2, 6)),
             pltpu.SemaphoreType.DMA((2, 6)),
-            pltpu.SemaphoreType.DMA((ROUNDS - 1, CHUNKS)),
-            pltpu.SemaphoreType.DMA((ROUNDS - 1, CHUNKS)),
+            pltpu.SemaphoreType.DMA((4, 2)),
+            pltpu.SemaphoreType.DMA((4, 2)),
+            pltpu.SemaphoreType.DMA((ROUNDS - 1, CHUNKS, 2)),
+            pltpu.SemaphoreType.DMA((ROUNDS - 1, CHUNKS, 2)),
             pltpu.SemaphoreType.DMA((6,)),
             pltpu.SemaphoreType.DMA((6,)),
         ],
         compiler_params=pltpu.CompilerParams(
             collective_id=0, has_side_effects=True, vmem_limit_bytes=60 * 1024 * 1024
         ),
-    )(recip, limbs, first, second, twiddle, third, third_back, second_back, first_back)
+    )(recip, limbs, first, second, twiddle, third, third_back, flip, second_back, first_back)
     return out.reshape(1, QUARTER * LANES)
 
 

time: 78.5 us -> 63.9 us (0.81)
  Pallas kernels: 76.8 us -> 62.2 us
    pallas_call x1, Pallas kernels: 76.8 us -> 62.2 us  [per_device(): pl.pallas_call(functools.partial(kernel, blocks), out_shape=jax.ShapeDtyp...]
where the time goes in v1:
time: 63.9 us; the launch traced here: 63.7 us
  Pallas kernels  62.2 us (97%)
  local copies, waits for them, and re-layouts  1.57 us (2%)
    pallas_call x1, Pallas kernels, per_device(): pl.pallas_call(functools.partial(kernel, blocks), out_shape=jax.ShapeDtyp...  62.2 us
    unnamed x1, local copies, waits for them, and re-layouts  1.57 us

profile of v1, /device:TPU:2, one launch (start us, length us, event | category | flops | bytes accessed | tf_op | source)
XLA Modules:
  0.0 63.7 jit_solution(432685935002269390)
XLA Ops:
  0.0 62.2 %shard_map.100 = f32[256,128]{1,0:T(8,128)} custom-call(f32[4096,128]{1,0:T(8,128)} %bitcast.7, f32[256,128]{1,0:T(8,128)} %bitcast.9, bf16[4,64,128]{2,1,0:T(8,128)(2,1)} %constant.16.clone.first_hbm, bf16[64,128,128]{2,1,0:T(8,128)(2,1)} %constant.17.clone.second_hbm, f32[64,2,32,128]{3,2,1,0:T(8,128)} %constant.18.clone.twiddle_hbm, ...), custom_call_target="tpu_custom_call" | custom-call | tf_op jit(solution)/shard_map/pallas_call | solution.py:510
  62.2 1.6 %copy.12 = f32[1,32768]{1,0:T(1,128)} copy(f32[1,32768]{1,0:T(1,128)} %bitcast.8) | data formatting | bytes 262144

commit v2 on v1

--- a/solution.py
+++ b/solution.py
@@ -23,6 +23,7 @@
 CHUNKS = ROWS // CHUNK
 ROUNDS = 4
 CORES = 2
+GROUP = 8
 CYCLE = 16
 
 
@@ -170,6 +171,7 @@
     first_back,
     mixed,
     spectra,
+    crossing,
     back,
     result,
     transit,
@@ -183,6 +185,9 @@
     share_recv,
     ring_send,
     ring_recv,
+    leave_send,
+    enter_send,
+    cross_recv,
     sum_send,
     sum_recv,
 ):
@@ -203,6 +208,14 @@
     mate = {"blk": blk + 1 - 2 * core, "acc": acc, "tail": tail}
     below = {"blk": blk - spot + lax.rem(spot + cycle - CORES, cycle), "acc": acc, "tail": tail}
     above = {"blk": blk - spot + lax.rem(spot + CORES, cycle), "acc": acc, "tail": tail}
+    crosses = blocks > cycle
+    makers = [spot == cycle - 1 - step for step in range(ROUNDS - 1)]
+    vias = [spot == 1, None, spot == cycle // 2 - 1]
+    to_via = [blocks - cycle + 2, None, cycle // 2 + 2]
+    to_start = [cycle - 1, 2, blocks - cycle // 2 + 1]
+
+    def along(steps):
+        return {"blk": lax.rem(blk + steps, blocks), "acc": acc, "tail": tail}
 
     def remote(src, dst, send_sem, recv_sem, device):
         return pltpu.make_async_remote_copy(
@@ -221,6 +234,31 @@
     barrier = pltpu.get_barrier_semaphore()
     for device in (right, left, later, earlier, onward, backward, below, above):
         pl.semaphore_signal(barrier, inc=1, device_id=device, device_id_type=pl.DeviceIdType.MESH)
+
+    def greet(steps):
+        pl.semaphore_signal(
+            barrier,
+            inc=1,
+            device_id=along(blocks - steps),
+            device_id_type=pl.DeviceIdType.MESH,
+        )
+
+    greeted = 8
+    if crosses:
+        for place in (*makers, vias[0], vias[2]):
+            greeted += jnp.where(place, 1, 0)
+
+        @pl.when(spot == 0)
+        def _():
+            for steps in to_start:
+                greet(steps)
+
+        for step in (0, 2):
+
+            @pl.when(vias[step])
+            def _():
+                greet(to_via[step])
+
     own_rows = pl.ds(acc * OWNED, ROWS)
     own_limbs = pltpu.make_async_copy(limbs_hbm, quarter(0, acc, 0, QUARTER), local_sem.at[0])
     local = [
@@ -242,7 +280,7 @@
         return carry
 
     lax.fori_loop(0, MID, clear, 0)
-    pl.semaphore_wait(barrier, 8)
+    pl.semaphore_wait(barrier, greeted)
 
     over = remote(
         quarter(0, acc, 0, QUARTER),
@@ -316,28 +354,80 @@
 
     lower = lax.broadcasted_iota(jnp.int32, (MID // 2, LANES), 1) < 64
 
-    def first_step(pair, carry):
-        values = [limbs[pl.ds(2 * pair + side, OUTER, stride=MID)] for side in range(2)]
+    def first_step(turn, carry):
+        values = [limbs[pl.ds(GROUP * turn + side, OUTER, stride=MID)] for side in range(GROUP)]
         product = left_product(first[...], jnp.concatenate(values, axis=1))
-        for side in range(2):
-            start = pl.multiple_of((2 * pair + side) * PADDED, PADDED)
+        for side in range(GROUP):
+            start = pl.multiple_of((GROUP * turn + side) * PADDED, PADDED)
             mixed[pl.ds(start, PADDED)] = product[:, side * LANES : (side + 1) * LANES]
         return carry
 
-    lax.fori_loop(0, MID // 2, first_step, 0)
+    lax.fori_loop(0, MID // GROUP, first_step, 0)
+
+    def chunk_of(step, chunk):
+        return spectra.at[step, :, pl.ds(chunk * CHUNK, CHUNK)]
 
     def ring(step, chunk):
-        rows = pl.ds(chunk * CHUNK, CHUNK)
-        return [
-            remote(
-                spectra.at[step, side, rows],
-                spectra.at[step + 1, side, rows],
-                ring_send.at[step, chunk, side],
-                ring_recv.at[step, chunk, side],
-                onward,
+        return remote(
+            chunk_of(step, chunk),
+            chunk_of(step + 1, chunk),
+            ring_send.at[step, chunk],
+            ring_recv.at[step, chunk],
+            onward,
+        )
+
+    def leave(step, chunk):
+        if vias[step] is None:
+            return remote(
+                chunk_of(0, chunk),
+                chunk_of(step + 1, chunk),
+                leave_send.at[chunk],
+                ring_recv.at[step, chunk],
+                along(to_start[step]),
             )
-            for side in range(2)
-        ]
+        return remote(
+            chunk_of(0, chunk),
+            crossing.at[:, pl.ds(chunk * CHUNK, CHUNK)],
+            leave_send.at[chunk],
+            cross_recv.at[chunk],
+            along(to_via[step]),
+        )
+
+    def enter(step, chunk):
+        return remote(
+            crossing.at[:, pl.ds(chunk * CHUNK, CHUNK)],
+            chunk_of(step + 1, chunk),
+            enter_send.at[chunk],
+            ring_recv.at[step, chunk],
+            along(to_start[step]),
+        )
+
+    def send_on(step, chunk):
+        if crosses:
+
+            @pl.when(jnp.logical_not(makers[0]))
+            def _():
+                ring(step, chunk).start()
+
+        else:
+            ring(step, chunk).start()
+
+    def send_across(chunk):
+        if crosses:
+            for step in range(ROUNDS - 1):
+
+                @pl.when(makers[step])
+                def _():
+                    leave(step, chunk).start()
+
+    def help_across(chunk):
+        if crosses:
+            for step in (0, 2):
+
+                @pl.when(vias[step])
+                def _():
+                    leave(step, chunk).wait_recv()
+                    enter(step, chunk).start()
 
     def forward(chunk, carry):
         reals, imags = [], []
@@ -363,8 +453,8 @@
             rows = product[place * MID : (place + 1) * MID]
             spectra[0, 0, chunk * CHUNK + place] = exchanged(rows[:, :LANES], lower)
             spectra[0, 1, chunk * CHUNK + place] = exchanged(rows[:, LANES:], lower)
-        for copy in ring(0, chunk):
-            copy.start()
+        send_across(chunk)
+        send_on(0, chunk)
         return carry
 
     lax.fori_loop(0, CHUNKS, forward, 0)
@@ -376,9 +466,10 @@
 
     def pass_ring(step):
         def body(chunk, carry):
-            for come, go in zip(ring(step, chunk), ring(step + 1, chunk)):
-                come.wait_recv()
-                go.start()
+            ring(step, chunk).wait_recv()
+            send_on(step + 1, chunk)
+            if step == 0:
+                help_across(chunk)
             return carry
 
         lax.fori_loop(0, CHUNKS, body, 0)
@@ -410,8 +501,7 @@
     lax.fori_loop(0, ROUNDS, weigh, 0)
 
     def arrive(chunk, carry):
-        for copy in ring(2, chunk):
-            copy.wait_recv()
+        ring(2, chunk).wait_recv()
         reals, imags = [], []
         for place in range(CHUNK):
             row = chunk * CHUNK + place
@@ -444,19 +534,19 @@
 
     lax.fori_loop(0, CHUNKS, arrive, 0)
 
-    def last_step(pair, carry):
+    def last_step(turn, carry):
         values = []
-        for side in range(2):
-            start = pl.multiple_of((2 * pair + side) * PADDED, PADDED)
+        for side in range(GROUP):
+            start = pl.multiple_of((GROUP * turn + side) * PADDED, PADDED)
             values.append(back[pl.ds(start, PADDED)])
         product = left_product(first_back[...], jnp.concatenate(values, axis=1))
-        for side in range(2):
-            result[pl.ds(2 * pair + side, MID, stride=MID)] = product[
+        for side in range(GROUP):
+            result[pl.ds(GROUP * turn + side, MID, stride=MID)] = product[
                 :, side * LANES : (side + 1) * LANES
             ]
         return carry
 
-    lax.fori_loop(0, MID // 2, last_step, 0)
+    lax.fori_loop(0, MID // GROUP, last_step, 0)
 
     def part(place, start):
         return result.at[pl.ds(place * QUARTER + start, HALF)]
@@ -491,9 +581,28 @@
         copy.wait_send()
 
     def drain(chunk, carry):
-        for step in range(ROUNDS - 1):
-            for copy in ring(step, chunk):
-                copy.wait_send()
+        if crosses:
+            for step in range(ROUNDS - 1):
+
+                @pl.when(makers[step])
+                def _():
+                    leave(step, chunk).wait_send()
+
+            for step in (0, 2):
+
+                @pl.when(vias[step])
+                def _():
+                    enter(step, chunk).wait_send()
+
+            @pl.when(jnp.logical_not(makers[0]))
+            def _():
+                for step in range(ROUNDS - 1):
+                    ring(step, chunk).wait_send()
+
+        else:
+            for step in range(ROUNDS - 1):
+                ring(step, chunk).wait_send()
+
         return carry
 
     lax.fori_loop(0, CHUNKS, drain, 0)
@@ -525,6 +634,7 @@
             pltpu.VMEM(first_back.shape[1:], jnp.bfloat16),
             pltpu.VMEM((MID * PADDED, LANES), jnp.float32),
             pltpu.VMEM((ROUNDS, 2, ROWS, MID, LANES), jnp.float32),
+            pltpu.VMEM((2, ROWS, MID, LANES), jnp.float32),
             pltpu.VMEM((MID * PADDED, LANES), jnp.float32),
             pltpu.VMEM((ACC * QUARTER, LANES), jnp.float32),
             pltpu.VMEM((2, HALF, LANES), jnp.float32),
@@ -536,8 +646,11 @@
             pltpu.SemaphoreType.DMA((2, 6)),
             pltpu.SemaphoreType.DMA((4, 2)),
             pltpu.SemaphoreType.DMA((4, 2)),
-            pltpu.SemaphoreType.DMA((ROUNDS - 1, CHUNKS, 2)),
-            pltpu.SemaphoreType.DMA((ROUNDS - 1, CHUNKS, 2)),
+            pltpu.SemaphoreType.DMA((ROUNDS - 1, CHUNKS)),
+            pltpu.SemaphoreType.DMA((ROUNDS - 1, CHUNKS)),
+            pltpu.SemaphoreType.DMA((CHUNKS,)),
+            pltpu.SemaphoreType.DMA((CHUNKS,)),
+            pltpu.SemaphoreType.DMA((CHUNKS,)),
             pltpu.SemaphoreType.DMA((6,)),
             pltpu.SemaphoreType.DMA((6,)),
         ],

time: 63.9 us -> 55.7 us (0.87)
  the two profiles are of different devices: /device:TPU:2 before, /device:TPU:1 now
where the time goes in v2:
time: 55.7 us; the launch traced here: 55.6 us
  Pallas kernels  54 us (97%)
  local copies, waits for them, and re-layouts  1.57 us (3%)
    pallas_call x1, Pallas kernels, per_device(): pl.pallas_call(functools.partial(kernel, blocks), out_shape=jax.ShapeDtyp...  54 us
    unnamed x1, local copies, waits for them, and re-layouts  1.57 us

profile of v2, /device:TPU:1, one launch (start us, length us, event | category | flops | bytes accessed | tf_op | source)
XLA Modules:
  0.0 55.6 jit_solution(6840201959465253185)
XLA Ops:
  0.0 54.0 %shard_map.100 = f32[256,128]{1,0:T(8,128)} custom-call(f32[4096,128]{1,0:T(8,128)} %bitcast.7, f32[256,128]{1,0:T(8,128)} %bitcast.9, bf16[4,64,128]{2,1,0:T(8,128)(2,1)} %constant.16.clone.first_hbm, bf16[64,128,128]{2,1,0:T(8,128)(2,1)} %constant.17.clone.second_hbm, f32[64,2,32,128]{3,2,1,0:T(8,128)} %constant.18.clone.twiddle_hbm, ...), custom_call_target="tpu_custom_call" | custom-call | tf_op jit(solution)/shard_map/pallas_call | solution.py:619
  54.0 1.6 %copy.12 = f32[1,32768]{1,0:T(1,128)} copy(f32[1,32768]{1,0:T(1,128)} %bitcast.8) | data formatting | bytes 262144

commit v3 on v2

--- a/solution.py
+++ b/solution.py
@@ -13,6 +13,9 @@
 ACC = 4
 OWNED = 16
 ROWS = 9
+LIMB_ROWS = 32
+PIECES = 2
+PIECE = 256 // PIECES
 PADDED = 32
 OUTER = 64
 MID = 32
@@ -49,40 +52,46 @@
     return np.cos(angle), np.sin(angle)
 
 
+def rows_of(place):
+    odd = place // 2
+    own = OWNED * place + 2 * np.arange(8) + odd
+    return np.append(own, own[0] if odd else OWNED * (ACC - 1 - place))
+
+
 @functools.lru_cache(maxsize=None)
 def tables():
-    rows = np.arange(OUTER)
-    limb = np.arange(OUTER)
+    rows = np.stack([rows_of(place) for place in range(ACC)])
+    limb = np.arange(LIMB_ROWS)
     mid = np.arange(MID)
     lane = np.arange(LANES)
     kappa = np.concatenate([np.arange(0, MID, 2), np.arange(1, MID, 2)])
     bins = 2 * (lane % 64) + lane // 64
     first, first_back = [], []
     for place in range(ACC):
-        own = rows[place * OWNED : place * OWNED + ROWS]
+        own = rows[place]
         real, imag = root(own[:, None] * limb[None, :], OUTER)
-        empty = np.zeros((PADDED - 2 * ROWS, OUTER))
+        empty = np.zeros((PADDED - 2 * ROWS, LIMB_ROWS))
         first.append(stacked_left(np.concatenate([real, imag, empty], axis=0)))
         order = [(place + 2) % ACC, (place + 1) % ACC, (place + 3) % ACC, place]
         kept = np.concatenate([np.arange(8 * q, 8 * q + 8) for q in order])
         real, imag = root(kept[:, None] * own[None, :], OUTER)
         empty = np.zeros((len(kept), PADDED - 2 * ROWS))
         first_back.append(stacked_left(np.concatenate([real, imag, empty], axis=1) / LENGTH))
-    freq = rows[:, None] + OUTER * kappa[None, :]
-    real, imag = root(freq[:, :, None] * mid[None, None, :], 2048)
+    freq = rows[:, :, None] + OUTER * kappa
+    real, imag = root(freq[..., None] * mid, 2048)
     second = stacked_left(
         np.concatenate(
-            [np.concatenate([real, -imag], axis=2), np.concatenate([imag, real], axis=2)], axis=1
+            [np.concatenate([real, -imag], axis=-1), np.concatenate([imag, real], axis=-1)], axis=-2
         )
     )
-    real, imag = real.transpose(0, 2, 1), -imag.transpose(0, 2, 1)
+    real, imag = real.swapaxes(-1, -2), -imag.swapaxes(-1, -2)
     second_back = stacked_left(
         np.concatenate(
-            [np.concatenate([real, -imag], axis=2), np.concatenate([imag, real], axis=2)], axis=1
+            [np.concatenate([real, -imag], axis=-1), np.concatenate([imag, real], axis=-1)], axis=-2
         )
     )
-    real, imag = root(freq[:, :, None] * lane[None, None, :], LENGTH)
-    twiddle = np.stack([real, imag], axis=1).astype(np.float32)
+    real, imag = root(freq[..., None] * lane, LENGTH)
+    twiddle = np.stack([real, imag], axis=2).astype(np.float32)
     real, imag = root(lane[:, None] * bins[None, :], LANES)
     third = np.stack(
         high_low(
@@ -153,20 +162,27 @@
     first_hbm,
     second_hbm,
     twiddle_hbm,
-    third_ref,
-    third_back_ref,
-    flip_ref,
+    third_hbm,
+    third_back_hbm,
+    flip_hbm,
     second_back_hbm,
     first_back_hbm,
     out_ref,
     recip,
     paired,
+    packed,
     flipped,
     weights,
+    own,
+    prior,
+    other,
     limbs,
     first,
     second,
     twiddle,
+    third,
+    third_back,
+    flip,
     second_back,
     first_back,
     mixed,
@@ -190,6 +206,7 @@
     cross_recv,
     sum_send,
     sum_recv,
+    ready,
 ):
     blk = lax.axis_index("blk")
     acc = lax.axis_index("acc")
@@ -200,11 +217,16 @@
     earlier = {"blk": lax.rem(blk + blocks - 1 + tail, blocks), "acc": acc, "tail": 1 - tail}
     onward = {"blk": lax.rem(blk + 1, blocks), "acc": acc, "tail": tail}
     backward = {"blk": lax.rem(blk + blocks - 1, blocks), "acc": acc, "tail": tail}
+    odd = acc // 2
+    pair = ACC - 1 - acc
+    twin = acc + 1 - 2 * lax.rem(acc, 2)
+    beside = {"blk": blk, "acc": twin, "tail": tail}
     partner = {"blk": blk, "acc": ACC - 1 - acc, "tail": tail}
     cycle = min(CYCLE, blocks)
     spot = lax.rem(blk, cycle)
     core = lax.rem(blk, CORES)
     parity = lax.rem(spot // CORES, 2)
+    across = {"blk": blk, "acc": acc, "tail": 1 - tail}
     mate = {"blk": blk + 1 - 2 * core, "acc": acc, "tail": tail}
     below = {"blk": blk - spot + lax.rem(spot + cycle - CORES, cycle), "acc": acc, "tail": tail}
     above = {"blk": blk - spot + lax.rem(spot + CORES, cycle), "acc": acc, "tail": tail}
@@ -227,12 +249,11 @@
             device_id_type=pl.DeviceIdType.MESH,
         )
 
-    def quarter(part, owner, start, size):
-        first_row = pl.multiple_of((part * ACC + owner) * QUARTER + start, HALF)
-        return limbs.at[pl.ds(first_row, size)]
+    def quarter(owner, piece):
+        return limbs.at[pl.ds(pl.multiple_of(owner * QUARTER + piece * PIECE, PIECE), PIECE)]
 
     barrier = pltpu.get_barrier_semaphore()
-    for device in (right, left, later, earlier, onward, backward, below, above):
+    for device in (right, left, earlier, backward, mate, across, below):
         pl.semaphore_signal(barrier, inc=1, device_id=device, device_id_type=pl.DeviceIdType.MESH)
 
     def greet(steps):
@@ -243,7 +264,7 @@
             device_id_type=pl.DeviceIdType.MESH,
         )
 
-    greeted = 8
+    greeted = 7
     if crosses:
         for place in (*makers, vias[0], vias[2]):
             greeted += jnp.where(place, 1, 0)
@@ -259,17 +280,20 @@
             def _():
                 greet(to_via[step])
 
-    own_rows = pl.ds(acc * OWNED, ROWS)
-    own_limbs = pltpu.make_async_copy(limbs_hbm, quarter(0, acc, 0, QUARTER), local_sem.at[0])
+    own_limbs = pltpu.make_async_copy(limbs_hbm, own, local_sem.at[0])
     local = [
         pltpu.make_async_copy(first_hbm.at[acc], first, local_sem.at[1]),
-        pltpu.make_async_copy(second_hbm.at[own_rows], second, local_sem.at[2]),
-        pltpu.make_async_copy(twiddle_hbm.at[own_rows], twiddle, local_sem.at[3]),
-        pltpu.make_async_copy(second_back_hbm.at[own_rows], second_back, local_sem.at[4]),
+        pltpu.make_async_copy(second_hbm.at[acc], second, local_sem.at[2]),
+        pltpu.make_async_copy(twiddle_hbm.at[acc], twiddle, local_sem.at[3]),
+        pltpu.make_async_copy(second_back_hbm.at[acc], second_back, local_sem.at[4]),
         pltpu.make_async_copy(first_back_hbm.at[acc], first_back, local_sem.at[5]),
-        pltpu.make_async_copy(recip_hbm, recip, local_sem.at[6]),
+        pltpu.make_async_copy(third_hbm, third, local_sem.at[7]),
+        pltpu.make_async_copy(third_back_hbm, third_back, local_sem.at[8]),
+        pltpu.make_async_copy(flip_hbm, flip, local_sem.at[9]),
     ]
+    own_recip = pltpu.make_async_copy(recip_hbm, recip, local_sem.at[6])
     own_limbs.start()
+    own_recip.start()
     for copy in local:
         copy.start()
     own_limbs.wait()
@@ -281,73 +305,88 @@
 
     lax.fori_loop(0, MID, clear, 0)
     pl.semaphore_wait(barrier, greeted)
-
-    over = remote(
-        quarter(0, acc, 0, QUARTER),
-        quarter(1, acc, 0, QUARTER),
-        over_send.at[0],
-        over_recv.at[0],
-        later,
-    )
-    over.start()
-
-    def gather(part, step, owner, start, device):
-        ref = quarter(part, owner, start, HALF)
-        return remote(ref, ref, gather_send.at[part, step], gather_recv.at[part, step], device)
-
-    from_left = lax.rem(acc + ACC - 1, ACC)
-    from_right = lax.rem(acc + 1, ACC)
-
-    def spread(part):
-        steps = [
-            gather(part, 0, acc, 0, right),
-            gather(part, 1, acc, HALF, left),
-            gather(part, 2, acc, HALF, right),
-            gather(part, 3, acc, 0, left),
-        ]
-        for copy in steps:
-            copy.start()
-        return steps
-
-    def pass_on(part, steps):
-        steps[0].wait_recv()
-        to_right = gather(part, 4, from_left, 0, right)
-        to_right.start()
-        steps[1].wait_recv()
-        to_left = gather(part, 5, from_right, HALF, left)
-        to_left.start()
-        return [to_right, to_left]
-
-    own_steps = spread(0)
-    over.wait_recv()
-    earlier_steps = spread(1)
-    own_steps += pass_on(0, own_steps)
-    earlier_steps += pass_on(1, earlier_steps)
-
-    def share(step, source, round_index, device):
-        found = []
-        for side in range(2):
-            start = pl.multiple_of(round_index * 1024 + side * 512 + 256, 256)
-            slot = paired.at[round_index, side]
-            found.append(
-                remote(
-                    recip_hbm.at[pl.ds(start, 256)] if source is None else slot,
-                    slot,
-                    share_send.at[step, side],
-                    share_recv.at[step, side],
-                    device,
-                )
-            )
-        return found
-
-    own_round = parity * 2 + core
-    fetched = share(0, None, own_round, partner)
-    to_mate = share(1, paired, own_round, mate)
-    to_below = share(2, paired, own_round, below)
-    relayed = share(3, paired, (1 - parity) * 2 + core, mate)
-    for copy in fetched:
+    pl.semaphore_signal(ready, inc=1, device_id=above, device_id_type=pl.DeviceIdType.MESH)
+
+    over = [
+        remote(
+            own.at[pl.ds(piece * PIECE, PIECE)],
+            prior.at[pl.ds(piece * PIECE, PIECE)],
+            over_send.at[piece],
+            over_recv.at[piece],
+            later,
+        )
+        for piece in range(PIECES)
+    ]
+    for copy in over:
         copy.start()
-    for copy in own_steps[2:] + earlier_steps[2:]:
+
+    def gather(step, piece, source, owner, device):
+        return remote(
+            source,
+            quarter(owner, piece),
+            gather_send.at[step, piece],
+            gather_recv.at[step, piece],
+            device,
+        )
+
+    pieces = range(PIECES)
+    to_pair = [
+        gather(0, piece, other.at[pl.ds(piece * PIECE, PIECE)], acc, partner) for piece in pieces
+    ]
+    to_twin = [gather(1, piece, quarter(acc, piece), acc, beside) for piece in pieces]
+    passed = [gather(2, piece, quarter(pair, piece), pair, beside) for piece in pieces]
+
+    def start_row(odd_row, row):
+        return (row // 4) * 256 + 2 * (row % 4) + odd_row
+
+    own_round = parity * 2 + tail
+    own_recip.wait()
+    for row in range(8):
+        start = own_round * 1024 + core * 512 + start_row(1 - odd, row)
+        packed[pl.ds(row, MID, stride=8)] = recip[pl.ds(start, MID, stride=8)]
+
+    def share(step, round_index, device):
+        slot = paired.at[round_index, core]
+        return remote(
+            packed if step == 0 else slot,
+            slot,
+            share_send.at[step],
+            share_recv.at[step],
+            device,
+        )
+
+    across_round = parity * 2 + 1 - tail
+    above_round = (1 - parity) * 2 + tail
+    far_round = (1 - parity) * 2 + 1 - tail
+    fetched = share(0, own_round, partner)
+    own_to_mate = share(1, own_round, mate)
+    own_across = share(2, own_round, across)
+    own_below = share(3, own_round, below)
+    across_to_mate = share(4, across_round, mate)
+    across_below = share(5, across_round, below)
+    above_to_mate = share(6, above_round, mate)
+    far_to_mate = share(7, far_round, mate)
+    fetched.start()
+    sign = (1 - 2 * odd).astype(jnp.float32)
+    for piece in pieces:
+        rows = pl.ds(piece * PIECE, PIECE)
+        over[piece].wait_recv()
+        signed = prior[rows] * sign
+        other[rows] = own[rows] - signed
+        to_pair[piece].start()
+        limbs[pl.ds(pl.multiple_of(acc * QUARTER + piece * PIECE, PIECE), PIECE)] = (
+            own[rows] + signed
+        )
+        to_twin[piece].start()
+    for piece in pieces:
+        to_pair[piece].wait_recv()
+        passed[piece].start()
+    fetched.wait_recv()
+    own_across.start()
+    pl.semaphore_wait(ready, 1)
+    own_below.start()
+    own_to_mate.start()
+    for copy in to_twin + passed:
         copy.wait_recv()
     for copy in local:
         copy.wait()
@@ -355,7 +394,7 @@
     lower = lax.broadcasted_iota(jnp.int32, (MID // 2, LANES), 1) < 64
 
     def first_step(turn, carry):
-        values = [limbs[pl.ds(GROUP * turn + side, OUTER, stride=MID)] for side in range(GROUP)]
+        values = [limbs[pl.ds(GROUP * turn + side, LIMB_ROWS, stride=MID)] for side in range(GROUP)]
         product = left_product(first[...], jnp.concatenate(values, axis=1))
         for side in range(GROUP):
             start = pl.multiple_of((GROUP * turn + side) * PADDED, PADDED)
@@ -363,6 +402,11 @@
         return carry
 
     lax.fori_loop(0, MID // GROUP, first_step, 0)
+    own_across.wait_recv()
+    across_below.start()
+    across_to_mate.start()
+    own_below.wait_recv()
+    above_to_mate.start()
 
     def chunk_of(step, chunk):
         return spectra.at[step, :, pl.ds(chunk * CHUNK, CHUNK)]
@@ -448,7 +492,7 @@
         value = jnp.concatenate(
             [jnp.concatenate(reals, axis=0), jnp.concatenate(imags, axis=0)], axis=1
         )
-        product = right_product(value, third_ref)
+        product = right_product(value, third)
         for place in range(CHUNK):
             rows = product[place * MID : (place + 1) * MID]
             spectra[0, 0, chunk * CHUNK + place] = exchanged(rows[:, :LANES], lower)
@@ -458,11 +502,10 @@
         return carry
 
     lax.fori_loop(0, CHUNKS, forward, 0)
-
-    for side in range(2):
-        fetched[side].wait_recv()
-        to_mate[side].start()
-        to_below[side].start()
+    across_below.wait_recv()
+    far_to_mate.start()
+    for copy in (own_to_mate, across_to_mate, above_to_mate, far_to_mate):
+        copy.wait_recv()
 
     def pass_ring(step):
         def body(chunk, carry):
@@ -474,31 +517,27 @@
 
         lax.fori_loop(0, CHUNKS, body, 0)
 
-    pass_ring(0)
-    for side in range(2):
-        to_below[side].wait_recv()
-        relayed[side].start()
-    pass_ring(1)
-    for side in range(2):
-        to_mate[side].wait_recv()
-        relayed[side].wait_recv()
-
     def weigh(step, carry):
         for side in range(2):
             high, low = split(paired[step, side])
-            turned = dot(jnp.concatenate([high, low], axis=1), flip_ref[...])
+            turned = dot(jnp.concatenate([high, low], axis=1), flip[...])
             for group in range(MID):
                 flipped[side, pl.ds((MID - 1 - group) * 8, 8)] = turned[group * 8 : group * 8 + 8]
             start = step * 1024 + side * 512
-            weights[step, side, 0] = recip[pl.ds(start, MID, stride=8)]
-            weights[step, side, ROWS - 1] = recip[pl.ds(start + 256, MID, stride=8)]
-            for row in range(1, ROWS - 1):
-                own = recip[pl.ds(start + row, MID, stride=8)]
-                other = flipped[side, pl.ds(8 - row, MID, stride=8)]
-                weights[step, side, row] = own + other if side == 0 else own - other
+            for row in range(ROWS - 1):
+                mine = recip[pl.ds(start + start_row(odd, row), MID, stride=8)]
+                mirrored = 7 if row == 0 else 8 - row - odd
+                theirs = flipped[side, pl.ds(mirrored, MID, stride=8)]
+                if row == 0:
+                    theirs = jnp.where(odd == 1, theirs, 0.0)
+                weights[step, side, row] = mine + theirs if side == 0 else mine - theirs
+            extra = paired[step, side, pl.ds(0, MID, stride=8)]
+            weights[step, side, ROWS - 1] = jnp.where(odd == 1, 0.0, extra)
         return carry
 
     lax.fori_loop(0, ROUNDS, weigh, 0)
+    pass_ring(0)
+    pass_ring(1)
 
     def arrive(chunk, carry):
         ring(2, chunk).wait_recv()
@@ -518,7 +557,7 @@
         value = jnp.concatenate(
             [jnp.concatenate(reals, axis=0), jnp.concatenate(imags, axis=0)], axis=1
         )
-        product = right_product(value, third_back_ref)
+        product = right_product(value, third_back)
         for place in range(CHUNK):
             row = chunk * CHUNK + place
             real = product[place * MID : (place + 1) * MID, :LANES]
@@ -559,7 +598,9 @@
     summed_left = remote(part(2, HALF), arrived.at[3], sum_send.at[5], sum_recv.at[5], left)
     to_right.start()
     to_left.start()
+    to_right.wait_send()
     plain_right.start()
+    to_left.wait_send()
     plain_left.start()
     to_right.wait_recv()
     result[QUARTER : QUARTER + HALF] += transit[0]
@@ -574,9 +615,10 @@
     summed_left.wait_recv()
     out_ref[HALF:] = result[3 * QUARTER + HALF :] + arrived[0] + arrived[3]
 
-    sent = [over, *own_steps, *earlier_steps]
-    sent += [*fetched, *to_mate, *to_below, *relayed]
-    sent += [to_right, to_left, plain_right, plain_left, summed_right, summed_left]
+    sent = [*over, *to_pair, *to_twin, *passed]
+    sent += [fetched, own_to_mate, own_across, own_below, across_to_mate, across_below]
+    sent += [above_to_mate, far_to_mate]
+    sent += [plain_right, plain_left, summed_right, summed_left]
     for copy in sent:
         copy.wait_send()
 
@@ -619,18 +661,23 @@
     out = pl.pallas_call(
         functools.partial(kernel, blocks),
         out_shape=jax.ShapeDtypeStruct((QUARTER, LANES), jnp.float32),
-        in_specs=[anywhere] * 5 + [vmem] * 3 + [anywhere] * 2,
+        in_specs=[anywhere] * 10,
         out_specs=vmem,
         scratch_shapes=[
             pltpu.VMEM((ROUNDS * 1024, LANES), jnp.float32),
             pltpu.VMEM((ROUNDS, 2, QUARTER, LANES), jnp.float32),
+            pltpu.VMEM((QUARTER, LANES), jnp.float32),
             pltpu.VMEM((2, QUARTER, LANES), jnp.float32),
             pltpu.VMEM((ROUNDS, 2, ROWS, MID, LANES), jnp.float32),
-            pltpu.VMEM((2 * ACC * QUARTER, LANES), jnp.float32),
+            *[pltpu.VMEM((QUARTER, LANES), jnp.float32)] * 3,
+            pltpu.VMEM((ACC * QUARTER, LANES), jnp.float32),
             pltpu.VMEM(first.shape[1:], jnp.bfloat16),
-            pltpu.VMEM((ROWS, *second.shape[1:]), jnp.bfloat16),
-            pltpu.VMEM((ROWS, *twiddle.shape[1:]), jnp.float32),
-            pltpu.VMEM((ROWS, *second_back.shape[1:]), jnp.bfloat16),
+            pltpu.VMEM(second.shape[1:], jnp.bfloat16),
+            pltpu.VMEM(twiddle.shape[1:], jnp.float32),
+            pltpu.VMEM(third.shape, jnp.bfloat16),
+            pltpu.VMEM(third_back.shape, jnp.bfloat16),
+            pltpu.VMEM(flip.shape, jnp.bfloat16),
+            pltpu.VMEM(second_back.shape[1:], jnp.bfloat16),
             pltpu.VMEM(first_back.shape[1:], jnp.bfloat16),
             pltpu.VMEM((MID * PADDED, LANES), jnp.float32),
             pltpu.VMEM((ROUNDS, 2, ROWS, MID, LANES), jnp.float32),
@@ -639,13 +686,13 @@
             pltpu.VMEM((ACC * QUARTER, LANES), jnp.float32),
             pltpu.VMEM((2, HALF, LANES), jnp.float32),
             pltpu.VMEM((4, HALF, LANES), jnp.float32),
-            pltpu.SemaphoreType.DMA((7,)),
-            pltpu.SemaphoreType.DMA((1,)),
-            pltpu.SemaphoreType.DMA((1,)),
-            pltpu.SemaphoreType.DMA((2, 6)),
-            pltpu.SemaphoreType.DMA((2, 6)),
-            pltpu.SemaphoreType.DMA((4, 2)),
-            pltpu.SemaphoreType.DMA((4, 2)),
+            pltpu.SemaphoreType.DMA((10,)),
+            pltpu.SemaphoreType.DMA((PIECES,)),
+            pltpu.SemaphoreType.DMA((PIECES,)),
+            pltpu.SemaphoreType.DMA((3, PIECES)),
+            pltpu.SemaphoreType.DMA((3, PIECES)),
+            pltpu.SemaphoreType.DMA((8,)),
+            pltpu.SemaphoreType.DMA((8,)),
             pltpu.SemaphoreType.DMA((ROUNDS - 1, CHUNKS)),
             pltpu.SemaphoreType.DMA((ROUNDS - 1, CHUNKS)),
             pltpu.SemaphoreType.DMA((CHUNKS,)),
@@ -653,6 +700,7 @@
             pltpu.SemaphoreType.DMA((CHUNKS,)),
             pltpu.SemaphoreType.DMA((6,)),
             pltpu.SemaphoreType.DMA((6,)),
+            pltpu.SemaphoreType.REGULAR,
         ],
         compiler_params=pltpu.CompilerParams(
             collective_id=0, has_side_effects=True, vmem_limit_bytes=60 * 1024 * 1024

time: 55.7 us -> 52 us (0.934)
  Pallas kernels: 54 us -> 49.8 us
    pallas_call x1, Pallas kernels: 54 us -> 49.8 us  [per_device(): pl.pallas_call(functools.partial(kernel, blocks), out_shape=jax.ShapeDtyp...]
where the time goes in v3:
time: 52 us; the launch traced here: 51.4 us
  Pallas kernels  49.8 us (96%)
  local copies, waits for them, and re-layouts  1.57 us (3%)
    pallas_call x1, Pallas kernels, per_device(): pl.pallas_call(functools.partial(kernel, blocks), out_shape=jax.ShapeDtyp...  49.8 us
    unnamed x1, local copies, waits for them, and re-layouts  1.57 us

profile of v3, /device:TPU:1, one launch (start us, length us, event | category | flops | bytes accessed | tf_op | source)
XLA Modules:
  0.0 51.4 jit_solution(8926529832314434581)
XLA Ops:
  0.0 49.8 %shard_map.100 = f32[256,128]{1,0:T(8,128)} custom-call(f32[4096,128]{1,0:T(8,128)} %bitcast.7, f32[256,128]{1,0:T(8,128)} %bitcast.9, bf16[4,64,64]{2,1,0:T(8,128)(2,1)} %constant.16.clone.first_hbm, bf16[4,9,128,128]{3,2,1,0:T(8,128)(2,1)} %constant.17.clone.second_hbm, f32[4,9,2,32,128]{4,3,2,1,0:T(8,128)} %constant.18.clone.twiddle_hbm, ...), custom_call_target="tpu_custom_call" | custom-call | tf_op jit(solution)/shard_map/pallas_call | solution.py:661
  49.8 1.6 %copy.12 = f32[1,32768]{1,0:T(1,128)} copy(f32[1,32768]{1,0:T(1,128)} %bitcast.8) | data formatting | bytes 262144

commit v4 on v3

--- a/solution.py
+++ b/solution.py
@@ -26,7 +26,7 @@
 CHUNKS = ROWS // CHUNK
 ROUNDS = 4
 CORES = 2
-GROUP = 8
+GROUP = 16
 CYCLE = 16
 
 
@@ -168,6 +168,7 @@
     second_back_hbm,
     first_back_hbm,
     out_ref,
+    more_ref,
     recip,
     paired,
     packed,
@@ -367,6 +368,14 @@
     above_to_mate = share(6, above_round, mate)
     far_to_mate = share(7, far_round, mate)
     fetched.start()
+
+    def pass_fetched():
+        fetched.wait_recv()
+        own_across.start()
+        own_to_mate.start()
+
+    late = jnp.logical_and(spot == 0, tail == 0)
+    pl.when(late)(pass_fetched)
     sign = (1 - 2 * odd).astype(jnp.float32)
     for piece in pieces:
         rows = pl.ds(piece * PIECE, PIECE)
@@ -381,11 +390,9 @@
     for piece in pieces:
         to_pair[piece].wait_recv()
         passed[piece].start()
-    fetched.wait_recv()
-    own_across.start()
+    pl.when(jnp.logical_not(late))(pass_fetched)
     pl.semaphore_wait(ready, 1)
     own_below.start()
-    own_to_mate.start()
     for copy in to_twin + passed:
         copy.wait_recv()
     for copy in local:
@@ -598,9 +605,7 @@
     summed_left = remote(part(2, HALF), arrived.at[3], sum_send.at[5], sum_recv.at[5], left)
     to_right.start()
     to_left.start()
-    to_right.wait_send()
     plain_right.start()
-    to_left.wait_send()
     plain_left.start()
     to_right.wait_recv()
     result[QUARTER : QUARTER + HALF] += transit[0]
@@ -608,17 +613,20 @@
     to_left.wait_recv()
     result[2 * QUARTER + HALF : 3 * QUARTER] += transit[1]
     summed_left.start()
+    out_ref[...] = result[3 * QUARTER :]
     plain_right.wait_recv()
+    out_ref[HALF:] += arrived[0]
     plain_left.wait_recv()
+    out_ref[:HALF] += arrived[1]
     summed_right.wait_recv()
-    out_ref[:HALF] = result[3 * QUARTER : 3 * QUARTER + HALF] + arrived[1] + arrived[2]
+    more_ref[:HALF] = arrived[2]
     summed_left.wait_recv()
-    out_ref[HALF:] = result[3 * QUARTER + HALF :] + arrived[0] + arrived[3]
+    more_ref[HALF:] = arrived[3]
 
     sent = [*over, *to_pair, *to_twin, *passed]
     sent += [fetched, own_to_mate, own_across, own_below, across_to_mate, across_below]
     sent += [above_to_mate, far_to_mate]
-    sent += [plain_right, plain_left, summed_right, summed_left]
+    sent += [to_right, to_left, plain_right, plain_left, summed_right, summed_left]
     for copy in sent:
         copy.wait_send()
 
@@ -658,11 +666,11 @@
     first, second, twiddle, third, third_back, second_back, first_back, flip = constants
     anywhere = pl.BlockSpec(memory_space=pl.ANY)
     vmem = pl.BlockSpec(memory_space=pltpu.VMEM)
-    out = pl.pallas_call(
+    kept, added = pl.pallas_call(
         functools.partial(kernel, blocks),
-        out_shape=jax.ShapeDtypeStruct((QUARTER, LANES), jnp.float32),
+        out_shape=[jax.ShapeDtypeStruct((QUARTER, LANES), jnp.float32)] * 2,
         in_specs=[anywhere] * 10,
-        out_specs=vmem,
+        out_specs=[vmem, vmem],
         scratch_shapes=[
             pltpu.VMEM((ROUNDS * 1024, LANES), jnp.float32),
             pltpu.VMEM((ROUNDS, 2, QUARTER, LANES), jnp.float32),
@@ -706,7 +714,7 @@
             collective_id=0, has_side_effects=True, vmem_limit_bytes=60 * 1024 * 1024
         ),
     )(recip, limbs, first, second, twiddle, third, third_back, flip, second_back, first_back)
-    return out.reshape(1, QUARTER * LANES)
+    return kept.reshape(1, QUARTER * LANES) + added.reshape(1, QUARTER * LANES)
 
 
 def solution(mesh):

time: 52 us -> 51.9 us (level)
  other arithmetic: 0 us -> 1.64 us
  local copies, waits for them, and re-layouts: 1.57 us -> 0 us
    add x0 -> x1, other arithmetic: none -> 1.64 us  [per_device(): return kept.reshape(1, QUARTER * LANES) + added.reshape(1, QUARTER * LANES)]
    unnamed x1 -> x0, local copies, waits for them, and re-layouts: 1.57 us -> none
where the time goes in v4:
time: 51.9 us; the launch traced here: 51 us
  Pallas kernels  49.4 us (95%)
  other arithmetic  1.64 us (3%)
    pallas_call x1, Pallas kernels, per_device(): pl.pallas_call(functools.partial(kernel, blocks), out_shape=[jax.ShapeDty...  49.4 us
    add x1, other arithmetic, per_device(): return kept.reshape(1, QUARTER * LANES) + added.reshape(1, QUARTER * LANES)  1.64 us

profile of v4, /device:TPU:1, one launch (start us, length us, event | category | flops | bytes accessed | tf_op | source)
XLA Modules:
  0.0 51.0 jit_solution(3345170336374503962)
XLA Ops:
  0.0 49.4 %shard_map.100 = (f32[256,128]{1,0:T(8,128)}, f32[256,128]{1,0:T(8,128)}) custom-call(f32[4096,128]{1,0:T(8,128)} %bitcast.7, f32[256,128]{1,0:T(8,128)} %bitcast.8, bf16[4,64,64]{2,1,0:T(8,128)(2,1)} %constant.16.clone.first_hbm, bf16[4,9,128,128]{3,2,1,0:T(8,128)(2,1)} %constant.17.clone.second_hbm, f32[4,9,2,32,128]{4,3,2,1,0:T(8,128)} %constant.18.clone.twiddle_hbm, ...), custom_call_target="tpu_custom_call" | custom-call | tf_op jit(solution)/shard_map/pallas_call | solution.py:669
  49.4 1.6 %add.14 = f32[256,128]{1,0:T(8,128)} add(f32[256,128]{1,0:T(8,128)} %get-tuple-element.7, f32[256,128]{1,0:T(8,128)} %get-tuple-element.8) | non-fusion elementwise | flops 32768 | bytes 393216 | tf_op jit(solution)/shard_map/add | solution.py:717

commit v5 on v4

--- a/solution.py
+++ b/solution.py
@@ -76,7 +76,10 @@
         kept = np.concatenate([np.arange(8 * q, 8 * q + 8) for q in order])
         real, imag = root(kept[:, None] * own[None, :], OUTER)
         empty = np.zeros((len(kept), PADDED - 2 * ROWS))
-        first_back.append(stacked_left(np.concatenate([real, imag, empty], axis=1) / LENGTH))
+        table = np.concatenate([real, imag, empty], axis=1) / LENGTH
+        first_back.append(
+            np.concatenate([stacked_left(table[:8]), stacked_left(table[8:])], axis=0)
+        )
     freq = rows[:, :, None] + OUTER * kappa
     real, imag = root(freq[..., None] * mid, 2048)
     second = stacked_left(
@@ -191,6 +194,7 @@
     crossing,
     back,
     result,
+    opposed,
     transit,
     arrived,
     local_sem,
@@ -580,40 +584,43 @@
 
     lax.fori_loop(0, CHUNKS, arrive, 0)
 
-    def last_step(turn, carry):
-        values = []
-        for side in range(GROUP):
-            start = pl.multiple_of((GROUP * turn + side) * PADDED, PADDED)
-            values.append(back[pl.ds(start, PADDED)])
-        product = left_product(first_back[...], jnp.concatenate(values, axis=1))
-        for side in range(GROUP):
-            result[pl.ds(GROUP * turn + side, MID, stride=MID)] = product[
-                :, side * LANES : (side + 1) * LANES
-            ]
-        return carry
-
-    lax.fori_loop(0, MID // GROUP, last_step, 0)
-
+    def unmix(table, target, count):
+        def body(turn, carry):
+            values = []
+            for side in range(GROUP):
+                start = pl.multiple_of((GROUP * turn + side) * PADDED, PADDED)
+                values.append(back[pl.ds(start, PADDED)])
+            product = left_product(table, jnp.concatenate(values, axis=1))
+            for side in range(GROUP):
+                target[pl.ds(GROUP * turn + side, count, stride=MID)] = product[
+                    :, side * LANES : (side + 1) * LANES
+                ]
+            return carry
+
+        lax.fori_loop(0, MID // GROUP, body, 0)
+
+    unmix(first_back[:16], opposed, 8)
     def part(place, start):
-        return result.at[pl.ds(place * QUARTER + start, HALF)]
-
-    to_right = remote(part(0, 0), transit.at[0], sum_send.at[0], sum_recv.at[0], right)
-    to_left = remote(part(0, HALF), transit.at[1], sum_send.at[1], sum_recv.at[1], left)
+        return result.at[pl.ds((place - 1) * QUARTER + start, HALF)]
+
+    to_right = remote(opposed.at[pl.ds(0, HALF)], transit.at[0], sum_send.at[0], sum_recv.at[0], right)
+    to_left = remote(opposed.at[pl.ds(HALF, HALF)], transit.at[1], sum_send.at[1], sum_recv.at[1], left)
     plain_right = remote(part(1, HALF), arrived.at[0], sum_send.at[2], sum_recv.at[2], right)
     plain_left = remote(part(2, 0), arrived.at[1], sum_send.at[3], sum_recv.at[3], left)
     summed_right = remote(part(1, 0), arrived.at[2], sum_send.at[4], sum_recv.at[4], right)
     summed_left = remote(part(2, HALF), arrived.at[3], sum_send.at[5], sum_recv.at[5], left)
     to_right.start()
     to_left.start()
+    unmix(first_back[16:], result, 24)
     plain_right.start()
     plain_left.start()
     to_right.wait_recv()
-    result[QUARTER : QUARTER + HALF] += transit[0]
+    result[:HALF] += transit[0]
     summed_right.start()
     to_left.wait_recv()
-    result[2 * QUARTER + HALF : 3 * QUARTER] += transit[1]
+    result[QUARTER + HALF : 2 * QUARTER] += transit[1]
     summed_left.start()
-    out_ref[...] = result[3 * QUARTER :]
+    out_ref[...] = result[2 * QUARTER :]
     plain_right.wait_recv()
     out_ref[HALF:] += arrived[0]
     plain_left.wait_recv()
@@ -691,7 +698,8 @@
             pltpu.VMEM((ROUNDS, 2, ROWS, MID, LANES), jnp.float32),
             pltpu.VMEM((2, ROWS, MID, LANES), jnp.float32),
             pltpu.VMEM((MID * PADDED, LANES), jnp.float32),
-            pltpu.VMEM((ACC * QUARTER, LANES), jnp.float32),
+            pltpu.VMEM(((ACC - 1) * QUARTER, LANES), jnp.float32),
+            pltpu.VMEM((QUARTER, LANES), jnp.float32),
             pltpu.VMEM((2, HALF, LANES), jnp.float32),
             pltpu.VMEM((4, HALF, LANES), jnp.float32),
             pltpu.SemaphoreType.DMA((10,)),

time: 51.9 us -> 51.6 us (level)
  no operation moved by 1% of the time
where the time goes in v5:
time: 51.6 us; the launch traced here: 50.8 us
  Pallas kernels  49.1 us (95%)
  other arithmetic  1.64 us (3%)
    pallas_call x1, Pallas kernels, per_device(): pl.pallas_call(functools.partial(kernel, blocks), out_shape=[jax.ShapeDty...  49.1 us
    add x1, other arithmetic, per_device(): return kept.reshape(1, QUARTER * LANES) + added.reshape(1, QUARTER * LANES)  1.64 us

profile of v5, /device:TPU:1, one launch (start us, length us, event | category | flops | bytes accessed | tf_op | source)
XLA Modules:
  0.0 50.8 jit_solution(6650934389561089302)
XLA Ops:
  0.0 49.1 %shard_map.100 = (f32[256,128]{1,0:T(8,128)}, f32[256,128]{1,0:T(8,128)}) custom-call(f32[4096,128]{1,0:T(8,128)} %bitcast.7, f32[256,128]{1,0:T(8,128)} %bitcast.8, bf16[4,64,64]{2,1,0:T(8,128)(2,1)} %constant.16.clone.first_hbm, bf16[4,9,128,128]{3,2,1,0:T(8,128)(2,1)} %constant.17.clone.second_hbm, f32[4,9,2,32,128]{4,3,2,1,0:T(8,128)} %constant.18.clone.twiddle_hbm, ...), custom_call_target="tpu_custom_call" | custom-call | tf_op jit(solution)/shard_map/pallas_call | solution.py:676
  49.1 1.6 %add.14 = f32[256,128]{1,0:T(8,128)} add(f32[256,128]{1,0:T(8,128)} %get-tuple-element.7, f32[256,128]{1,0:T(8,128)} %get-tuple-element.8) | non-fusion elementwise | flops 32768 | bytes 393216 | tf_op jit(solution)/shard_map/add | solution.py:725

commit v6 on v5

--- a/solution.py
+++ b/solution.py
@@ -26,7 +26,7 @@
 CHUNKS = ROWS // CHUNK
 ROUNDS = 4
 CORES = 2
-GROUP = 16
+GROUP = 32
 CYCLE = 16
 
 

time: 51.6 us -> 51.5 us (level)
  no operation moved by 1% of the time
where the time goes in v6:
time: 51.5 us; the launch traced here: 50.8 us
  Pallas kernels  49.2 us (96%)
  other arithmetic  1.64 us (3%)
    pallas_call x1, Pallas kernels, per_device(): pl.pallas_call(functools.partial(kernel, blocks), out_shape=[jax.ShapeDty...  49.2 us
    add x1, other arithmetic, per_device(): return kept.reshape(1, QUARTER * LANES) + added.reshape(1, QUARTER * LANES)  1.64 us

profile of v6, /device:TPU:1, one launch (start us, length us, event | category | flops | bytes accessed | tf_op | source)
XLA Modules:
  0.0 50.8 jit_solution(4555518708602126255)
XLA Ops:
  0.0 49.2 %shard_map.100 = (f32[256,128]{1,0:T(8,128)}, f32[256,128]{1,0:T(8,128)}) custom-call(f32[4096,128]{1,0:T(8,128)} %bitcast.7, f32[256,128]{1,0:T(8,128)} %bitcast.8, bf16[4,64,64]{2,1,0:T(8,128)(2,1)} %constant.16.clone.first_hbm, bf16[4,9,128,128]{3,2,1,0:T(8,128)(2,1)} %constant.17.clone.second_hbm, f32[4,9,2,32,128]{4,3,2,1,0:T(8,128)} %constant.18.clone.twiddle_hbm, ...), custom_call_target="tpu_custom_call" | custom-call | tf_op jit(solution)/shard_map/pallas_call | solution.py:676
  49.2 1.6 %add.14 = f32[256,128]{1,0:T(8,128)} add(f32[256,128]{1,0:T(8,128)} %get-tuple-element.7, f32[256,128]{1,0:T(8,128)} %get-tuple-element.8) | non-fusion elementwise | flops 32768 | bytes 393216 | tf_op jit(solution)/shard_map/add | solution.py:725
